TPU v7x, 256 devices: a whole 4x4x8 slice. The times are simulated.
256 devices in a mesh: fsdp: 32 (over z, y_lo, core), ctx: 8 (over x, y_hi).
Axes of the slice: x: 4, y: 4 (y_hi: 2, y_lo: 2; y = y_hi * 2 + y_lo), z: 8, core: 2. Of those that a mesh axis runs over, the one named last changes fastest.
Arguments:
- hidden: bfloat16 [32, 2048, 5120], P('fsdp', 'ctx'), may hold values from -6 to 6
- queries: bfloat16 [32, 2048, 4096], P('fsdp', 'ctx'), may hold values from -300 to 300, as said below
- norm_gain: float32 [5120], replicated, may hold values from 0.1 to 1.9
- key_gain: float32 [128], replicated, may hold values from 0.1 to 1.9
- k_weight: bfloat16 [5120, 512], P('fsdp'), may hold values from -0.078125 to 0.078125
- v_weight: bfloat16 [5120, 512], P('fsdp'), may hold values from -0.078125 to 0.078125
- segment: int32 [32, 2048], P('fsdp', 'ctx'), may hold values from 0 to 3, as said below
- position: int32 [32, 2048], P('fsdp', 'ctx'), may hold values from 0 to 8191, as said below
Outputs:
- attended: bfloat16 [32, 2048, 4096], P('fsdp', 'ctx')
Inputs may be any that keep to these rules, and one draw needn't show every extreme that they name: queries keep to the stated range. `segment`: in each stretch, read in the tokens' order, rollout numbers never fall; the tokens of a stretch lie in its slots in an order that keeps 256 slots on each index of ctx, one token of every 8 consecutive ones on each. `position`: within one rollout of a stretch positions rise by one from token to token.
All inputs are finite; a program needn't handle non-finite values.
Results may differ from a plain program's by a relative error of at most 0.0075.
The roundings to bfloat16 on the way count: a program that leaves them out, or rounds other values in their place, can miss the bound.
Values may be sent and summed in bfloat16 or wider, within the bound.
A program may use at most 192 MiB of HBM per device.

v0:
```python
import math

import jax
import jax.numpy as jnp
from jax import lax
from jax.sharding import PartitionSpec as P

KVH = 4
HD = 128
G = 8


EPS = 1e-06
THETA = 1000000.0


def rotate(values_in, where):
    width = values_in.shape[-1]
    half = width // 2
    freq = jnp.exp(jnp.arange(half, dtype=jnp.float32) * (-2.0 * math.log(THETA) / width))
    angle = where.astype(jnp.float32)[:, None] * freq[None, :]
    cosine = jnp.cos(angle)[:, None, :]
    sine = jnp.sin(angle)[:, None, :]
    first = values_in[..., :half]
    second = values_in[..., half:]
    return jnp.concatenate(
        [first * cosine - second * sine, second * cosine + first * sine], axis=-1
    )


def on_device(hidden, queries, norm_gain, key_gain, k_weight, v_weight, segment, position):
    rows_here = hidden.shape[1]
    inputs = hidden[0].astype(jnp.float32)
    normed = (
        inputs * lax.rsqrt(jnp.mean(inputs * inputs, axis=-1, keepdims=True) + EPS) * norm_gain
    ).astype(jnp.bfloat16)
    key_sums = jnp.dot(
        normed,
        lax.all_gather(k_weight, "fsdp", axis=0, tiled=True),
        preferred_element_type=jnp.float32,
    )
    value_sums = jnp.dot(
        normed,
        lax.all_gather(v_weight, "fsdp", axis=0, tiled=True),
        preferred_element_type=jnp.float32,
    )
    raw = key_sums.reshape(rows_here, KVH, HD)
    normk = raw * lax.rsqrt(jnp.mean(raw * raw, axis=-1, keepdims=True) + EPS) * key_gain
    keys = rotate(normk, position[0]).astype(jnp.bfloat16)
    values = value_sums.reshape(rows_here, KVH, HD).astype(jnp.bfloat16)
    grouped = queries[0].reshape(rows_here, KVH, G, HD)
    own_seg = segment[0]
    own_pos = position[0]
    scale = 1.0 / math.sqrt(HD)
    running = jnp.full((KVH, G, rows_here), -1e30, jnp.float32)
    key_piece = lax.all_gather(keys[None], "ctx", axis=1, tiled=True)
    value_piece = lax.all_gather(values[None], "ctx", axis=1, tiled=True)
    seg_piece = lax.all_gather(segment, "ctx", axis=1, tiled=True)
    pos_piece = lax.all_gather(position, "ctx", axis=1, tiled=True)
    scores = (
        jnp.einsum("tkgd,skd->kgts", grouped, key_piece[0], preferred_element_type=jnp.float32)
        * scale
    )
    allowed = (seg_piece[0][None, :] == own_seg[:, None]) & (
        pos_piece[0][None, :] <= own_pos[:, None]
    )
    scores = jnp.where(allowed, scores, -1e30)
    newest = jnp.maximum(running, jnp.max(scores, axis=-1))
    weights = jnp.where(allowed, jnp.exp(scores - newest[..., None]), 0.0)
    rounded = weights.astype(jnp.bfloat16)
    total = jnp.sum(weights, axis=-1)
    summed = jnp.einsum(
        "kgts,skd->kgtd", rounded, value_piece[0], preferred_element_type=jnp.float32
    )
    running, total, summed = (newest, total, summed)
    result = summed / total[..., None]
    result = (
        jnp.transpose(result, (2, 0, 1, 3)).reshape(rows_here, KVH * G * HD).astype(jnp.bfloat16)
    )
    return result[None]


def solution(mesh):
    placed = (
        P("fsdp", "ctx", None),
        P("fsdp", "ctx", None),
        P(),
        P(),
        P("fsdp", None),
        P("fsdp", None),
        P("fsdp", "ctx"),
        P("fsdp", "ctx"),
    )
    return jax.shard_map(
        on_device, mesh=mesh, in_specs=placed, out_specs=P("fsdp", "ctx", None), check_vma=False
    )
```

profile of v0, /device:TPU:1, one launch (start us, length us, event | category | flops | bytes accessed | tf_op | source)
XLA Modules:
  0.0 313.9 jit_solution(9623700684279206737)
XLA Ops:
  6.5 0.0 all-gather.6.cloned.1.call-start
  6.5 0.7 all-gather.6.cloned.1.call-update
  7.3 0.0 all-gather.10.cloned.1.call-start
  7.3 0.7 all-gather.10.cloned.1.call-update
  8.0 0.0 all-gather.8.cloned.1.call-start
  8.1 0.7 convert_element_type.50
  8.7 2.3 fusion.6
  11.1 0.3 multiply_cosine_fusion
  11.4 70.2 %all-gather.6.cloned.1.call-done = bf16[5120,512]{1,0:T(8,128)(2,1)} async-done(((bf16[160,512]{1,0:T(8,128)(2,1)}), bf16[5120,512]{1,0:T(8,128)(2,1)}) %all-gather.6.cloned.1.call-update) | async-done | bytes 5242896 | tf_op jit(solution)/shard_map/all_gather | solution.py:39
  81.7 0.0 copy-start
  81.7 0.0 copy-start.4
  81.7 8.1 %copy.9 = bf16[512,5120]{1,0:T(8,128)(2,1)} copy(bf16[512,5120]{0,1:T(8,128)(2,1)} %bitcast.66) | data formatting | bytes 10485760 | tf_op jit(solution)/shard_map/dot_general | solution.py:37
  89.8 0.0 copy-done
  89.8 0.0 copy-done.4
  89.8 0.0 copy-start.3
  89.8 4.2 %multiply_reduce_fusion = (f32[256,4]{0,1:T(4,128)S(1)}, f32[256,4,128]{0,2,1:T(8,128)S(1)}) fusion(bf16[4,128,5120]{2,1,0:T(8,128)(2,1)} %bitcast.67, bf16[1,256,5120]{2,1,0:T(8,128)(2,1)S(1)} %copy-done, f32[5120]{0:T(1024)S(1)} %copy-done.4, f32[256]{0:T(256)S(1)} %add_rsqrt_fusion.1), kind=kOutput, calls=%fused_computation.26 | convolution fusion | flops 1347681280 | bytes 8414208 | tf_op jit(solution)/shard_map/dot_general | solution.py:37
  94.0 0.0 copy-start.1
  94.0 0.0 copy-start.2
  94.0 0.0 copy-done.3
  94.0 0.1 multiply_multiply_fusion
  94.1 0.1 fusion.26
  94.2 0.7 pad_maximum_fusion
  94.9 0.0 all-gather.8.cloned.1.call-update
  94.9 0.0 all-gather.12.cloned.1.call-start
  95.0 2.1 copy.21
  97.1 0.0 copy-done.1
  97.1 19.3 %all_gather.19 = s32[1,2048]{1,0:T(1,128)S(1)} all-gather(s32[1,256]{1,0:T(1,128)S(1)} %copy-done.1), channel_id=1, replica_groups=mesh['fsdp'=32,'ctx'=8] {'ctx'}, dimensions={1}, use_global_device_ids=true | all-gather | bytes 9216 | tf_op jit(solution)/shard_map/all_gather | solution.py:59
  116.4 0.0 copy-done.2
  116.4 14.8 %all_gather.18 = s32[1,2048]{1,0:T(1,128)S(1)} all-gather(s32[1,256]{1,0:T(1,128)S(1)} %copy-done.2), channel_id=1, replica_groups=mesh['fsdp'=32,'ctx'=8] {'ctx'}, dimensions={1}, use_global_device_ids=true | all-gather | bytes 9216 | tf_op jit(solution)/shard_map/all_gather | solution.py:58
  131.2 1.4 compare_and_fusion
  132.6 19.0 %all-gather.10.cloned.1.call-done = bf16[5120,512]{1,0:T(8,128)(2,1)} async-done(((bf16[160,512]{1,0:T(8,128)(2,1)}), bf16[5120,512]{1,0:T(8,128)(2,1)}) %all-gather.10.cloned.1.call-update) | async-done | bytes 5242896 | tf_op jit(solution)/shard_map/all_gather | solution.py:44
  151.6 6.3 %fusion.20 = bf16[256,4,128]{0,2,1:T(8,128)(2,1)} fusion(bf16[1,256,5120]{2,1,0:T(8,128)(2,1)} %param.8, f32[5120]{0:T(1024)S(1)} %copy-done.4, f32[256]{0:T(256)S(1)} %add_rsqrt_fusion.1, bf16[5120,512]{1,0:T(8,128)(2,1)} %all-gather.10.cloned.1.call-done), kind=kOutput, calls=%fused_computation.23 | convolution fusion | flops 1347551232 | bytes 8147968 | tf_op jit(solution)/shard_map/dot_general | solution.py:42
  158.0 0.0 all-gather.12.cloned.1.call-update
  158.0 57.2 %all-gather.8.cloned.1.call-done = bf16[1,2048,4,128]{1,3,2,0:T(8,128)(2,1)} async-done(((bf16[1,256,4,128]{1,3,2,0:T(8,128)(2,1)}), bf16[1,2048,4,128]{1,3,2,0:T(8,128)(2,1)}) %all-gather.8.cloned.1.call-update) | async-done | bytes 2097168 | tf_op jit(solution)/shard_map/all_gather | solution.py:56
  215.2 26.0 %fusion = (f32[4,8,256]{2,1,0:T(8,128)S(1)}, f32[4,2048,256,8]{2,1,3,0:T(8,128)}) fusion(pred[256,2048]{0,1:T(8,128)(4,1)S(1)} %compare_and_fusion, bf16[256,4,8,128]{3,2,1,0:T(8,128)(2,1)S(1)} %bitcast.65, bf16[1,2048,4,128]{1,3,2,0:T(8,128)(2,1)} %all-gather.8.cloned.1.call-done), kind=kOutput, calls=%fused_computation.2 | convolution fusion | flops 4345290752 | bytes 71860224 | tf_op jit(solution)/shard_map/tkgd,skd->kgts/dot_general | solution.py:61
  241.1 22.0 %fusion.1 = f32[4,8,256]{2,1,0:T(8,128)S(1)} fusion(f32[4,2048,256,8]{2,1,3,0:T(8,128)} %get-tuple-element.12, f32[4,8,256]{2,1,0:T(8,128)S(1)} %broadcast_maximum_fusion, pred[256,2048]{0,1:T(8,128)(4,1)S(1)} %compare_and_fusion), kind=kLoop, calls=%fused_computation.3 | loop fusion | flops 83877888 | bytes 67698688 | tf_op jit(solution)/shard_map/reduce_sum | solution.py:71
  263.1 15.9 %all-gather.12.cloned.1.call-done = bf16[2048,4,128]{0,2,1:T(8,128)(2,1)} async-done(((bf16[256,4,128]{0,2,1:T(8,128)(2,1)}), bf16[2048,4,128]{0,2,1:T(8,128)(2,1)}) %all-gather.12.cloned.1.call-update) | async-done | bytes 2097168 | tf_op jit(solution)/shard_map/all_gather | solution.py:57
  279.0 25.5 %fusion.12 = bf16[256,4,8,128]{0,3,2,1:T(8,128)(2,1)S(1)} fusion(f32[4,2048,256,8]{2,1,3,0:T(8,128)} %get-tuple-element.12, f32[4,8,256]{2,1,0:T(8,128)S(1)} %broadcast_maximum_fusion, pred[256,2048]{0,1:T(8,128)(4,1)S(1)} %compare_and_fusion, bf16[2048,4,128]{0,2,1:T(8,128)(2,1)} %all-gather.12.cloned.1.call-done, f32[256,4,8]{0,2,1:T(8,128)S(1)} %bitcast.70), kind=kOutput, calls=%fused_computation.16 | convolution fusion | flops 4380950528 | bytes 71892992 | tf_op jit(solution)/shard_map/kgts,skd->kgtd/dot_general | solution.py:72
  304.5 2.9 copy.13
  (4 shorter events, 0.0 us)
Async XLA Ops:
  6.5 75.1 %all-gather.6.cloned.1.call-start = ((), (), s32[]{:S(2)}) async-start(), calls=%async_computation | async-start | bytes 5406720 | tf_op jit(solution)/shard_map/all_gather | solution.py:39
  7.3 144.4 %all-gather.10.cloned.1.call-start = ((), (), s32[]{:S(2)}) async-start(), calls=%async_computation.2 | async-start | bytes 5406720 | tf_op jit(solution)/shard_map/all_gather | solution.py:44
  8.0 207.2 %all-gather.8.cloned.1.call-start = ((), (), s32[]{:S(2)}) async-start(), calls=%async_computation.1 | async-start | bytes 2359296 | tf_op jit(solution)/shard_map/all_gather | solution.py:56
  81.7 8.1 %copy-start = (bf16[1,256,5120]{2,1,0:T(8,128)(2,1)S(1)}, bf16[1,256,5120]{2,1,0:T(8,128)(2,1)}, u32[]{:S(2)}) copy-start(bf16[1,256,5120]{2,1,0:T(8,128)(2,1)} %param.8) | copy-start | bytes 7864324
  81.7 8.1 %copy-start.4 = (f32[5120]{0:T(1024)S(1)}, f32[5120]{0:T(1024)}, u32[]{:S(2)}) copy-start(f32[5120]{0:T(1024)} %param.10) | copy-start | bytes 61444
  89.8 4.2 %copy-start.3 = (f32[128]{0:T(128)S(1)}, f32[128]{0:T(128)}, u32[]{:S(2)}) copy-start(f32[128]{0:T(128)} %param.11) | copy-start | bytes 1540
  94.0 3.1 copy-start.1
  94.0 22.4 %copy-start.2 = (s32[1,256]{1,0:T(1,128)S(1)}, s32[1,256]{1,0:T(1,128)}, u32[]{:S(2)}) copy-start(s32[1,256]{1,0:T(1,128)} %param.14) | copy-start | bytes 3076
  94.9 184.1 %all-gather.12.cloned.1.call-start = ((), (), s32[]{:S(2)}) async-start(), calls=%async_computation.3 | async-start | bytes 2359296 | tf_op jit(solution)/shard_map/all_gather | solution.py:57
Sparse Core Ops, SparseCore 0:
  9.2 72.4 all-gather.5
  83.5 68.0 all-gather.9
  154.1 61.0 all-gather.7
  217.5 61.4 all-gather.11
where the time goes:
time: 314 us
  waiting for transfers between devices  164 us (52%)
  matrix products  62 us (20%)
  blocking collectives  34.1 us (11%)
  other arithmetic  27.7 us (9%)
  between operations  13.2 us (4%)
  local copies, waits for them, and re-layouts  13.1 us (4%)
    all_gather x1, waiting for transfers between devices, on_device(): lax.all_gather(k_weight, 'fsdp', axis=0, tiled=True)  70.2 us
    all_gather x1, waiting for transfers between devices, on_device(): key_piece = lax.all_gather(keys[None], 'ctx', axis=1, tiled=True)  57.2 us
    dot_general x1, matrix products, on_device(): jnp.einsum('tkgd,skd->kgts', grouped, key_piece[0], preferred_element_typ...  26 us
    dot_general x1, matrix products, on_device(): jnp.einsum('kgts,skd->kgtd', rounded, value_piece[0], preferred_element_t...  25.5 us
    reduce_sum x1, other arithmetic, on_device(): total = jnp.sum(weights, axis=-1)  22 us
    all_gather x1, blocking collectives, on_device(): pos_piece = lax.all_gather(position, 'ctx', axis=1, tiled=True)  19.3 us
    all_gather x1, waiting for transfers between devices, on_device(): lax.all_gather(v_weight, 'fsdp', axis=0, tiled=True)  19 us
    all_gather x1, waiting for transfers between devices, on_device(): value_piece = lax.all_gather(values[None], 'ctx', axis=1, tiled=True)  15.9 us
  transfers between devices with their start and end apart: 4, of which 4 were waited for; matrix products, arithmetic and copies ran while one was open for 24% of the time, Pallas kernels for 0%

commit v1 on v0

v1 whole, which is shorter than its diff:
```python
import functools
import math

import jax
import jax.numpy as jnp
from jax import lax
from jax.experimental import pallas as pl
from jax.experimental.pallas import tpu as pltpu
from jax.sharding import PartitionSpec as P

KVH = 4
HD = 128
G = 8
GROUPS = 8
EPS = 1e-06
THETA = 1000000.0
BIG = 8192
NEG = -1e30
X, Y, Z = 4, 4, 8
MESH = pl.DeviceIdType.MESH


def place():
    f = lax.axis_index("fsdp")
    c = lax.axis_index("ctx")
    return c // 2, (c % 2) * 2 + (f // 2) % 2, f // 4, f % 2


def device(x, y, z, core):
    x, y, z = (x + X) % X, (y + Y) % Y, (z + Z) % Z
    return {"fsdp": (z * 2 + y % 2) * 2 + core, "ctx": x * 2 + y // 2}


def gather_kernel(
    hidden_ref, gain_ref, key_gain_ref, cos_ref, sin_ref, code_ref, kw_ref, vw_ref,
    kv_ref, codes_ref,
    wbuf, normed, kv, codes,
    z_send, z_recv, y_send, y_recv, d_send, d_recv, kv_send, kv_recv, c_send, c_recv, out_sem,
):
    x, y, z, core = place()
    ylo, yhi = y % 2, y // 2
    ctx = x * 2 + yhi
    sgn = 1 - 2 * core
    rows = kw_ref.shape[0]
    width = 2 * HD
    tokens = hidden_ref.shape[0]
    half = tokens // 2

    peers = [(x + dx, y + dy, z, core) for dx in range(X) for dy in (0, 2) if (dx, dy) != (0, 0)]
    near = [(x, y, z + 1, core), (x, y, z - 1, core), (x, y + 1, z, core), (x, y - 1, z, core), (x, y, z, 1 - core)]
    barrier = pltpu.get_barrier_semaphore()
    for at in peers + near:
        pl.semaphore_signal(barrier, inc=1, device_id=device(*at), device_id_type=MESH)

    for h in range(KVH):
        wbuf[h, z, ylo, core, :, :HD] = kw_ref[:, h * HD:(h + 1) * HD]
        wbuf[h, z, ylo, core, :, HD:] = vw_ref[:, h * HD:(h + 1) * HD]
    codes[ctx] = code_ref[...]
    pl.semaphore_wait(barrier, len(peers + near))

    sent = []

    def send(src, dst, ssem, rsem, at):
        copy = pltpu.make_async_remote_copy(
            src_ref=src, dst_ref=dst, send_sem=ssem, recv_sem=rsem, device_id=device(*at), device_id_type=MESH)
        copy.start()
        sent.append(copy)

    def arrived(dst, ssem, rsem):
        pltpu.make_async_remote_copy(
            src_ref=dst, dst_ref=dst, send_sem=ssem, recv_sem=rsem, device_id=device(x, y, z, 1 - core),
            device_id_type=MESH).wait_recv()

    def slab(h, zz, yl, cc):
        return wbuf.at[h, (zz + 2 * Z) % Z, yl, cc]

    def ring(h, way, step):
        zz = z - sgn * step if way == 0 else z + sgn * step
        to = z + sgn if way == 0 else z - sgn
        block = slab(h, zz, ylo, core)
        if step > 0:
            arrived(block, z_send.at[h, way, step - 1], z_recv.at[h, way, step - 1])
        if step < (4 if way == 0 else 3):
            send(block, block, z_send.at[h, way, step], z_recv.at[h, way, step], (x, y, to, core))
        if way == 1 or step > 0:
            k = (step - 1) if way == 0 else 4 + step
            send(block, block, y_send.at[h, k], y_recv.at[h, k], (x, y + sgn if way == 0 else y - sgn, z, core))

    def w_start(h):
        ring(h, 0, 0)
        ring(h, 1, 0)

    def w_step(h, s):
        ring(h, 0, s)
        if s < 4:
            ring(h, 1, s)
        if s == 4:
            own = wbuf.at[h, :, ylo, core]
            send(own, own, d_send.at[h, 0], d_recv.at[h, 0], (x, y, z, 1 - core))

    def w_other(h):
        for k in range(8):
            zz = z - sgn * (k + 1) if k < 4 else z + sgn * (k - 4)
            arrived(slab(h, zz, 1 - ylo, core), y_send.at[h, k], y_recv.at[h, k])
        own = wbuf.at[h, :, 1 - ylo, core]
        send(own, own, d_send.at[h, 1], d_recv.at[h, 1], (x, y, z, 1 - core))

    def kv_send_to(h, n, block, at):
        send(block, block, kv_send.at[h, n], kv_recv.at[h, n], at)

    def kv_arrived(h, n, block):
        arrived(block, kv_send.at[h, n], kv_recv.at[h, n])

    def project(h):
        arrived(wbuf.at[h, :, ylo, 1 - core], d_send.at[h, 0], d_recv.at[h, 0])
        arrived(wbuf.at[h, :, 1 - ylo, 1 - core], d_send.at[h, 1], d_recv.at[h, 1])
        sums = jnp.zeros((tokens, width), jnp.float32)
        deep = 4 * rows
        for n in range(Z):
            sums += jnp.dot(normed[:, n * deep:(n + 1) * deep], wbuf[h, n].reshape(deep, width), preferred_element_type=jnp.float32)
        raw = sums[:, :HD]
        normk = raw * lax.rsqrt(jnp.mean(raw * raw, axis=-1, keepdims=True) + EPS) * key_gain_ref[...]
        turned = jnp.concatenate([normk[:, HD // 2:], normk[:, :HD // 2]], axis=1)
        kv[h, ctx, :, :HD] = (normk * cos_ref[...] + turned * sin_ref[...]).astype(jnp.bfloat16)
        kv[h, ctx, :, HD:] = sums[:, HD:].astype(jnp.bfloat16)
        block = kv.at[h, ctx]
        kv_send_to(h, 0, block, (x, y + 2, z, core))
        kv_send_to(h, 1, block, (x + 1, y, z, core))
        kv_send_to(h, 2, block, (x - 1, y, z, core))

    def spread(h, yh, base):
        left = ((x + X - 1) % X) * 2 + yh
        right = ((x + 1) % X) * 2 + yh
        kv_arrived(h, base, kv.at[h, left])
        kv_send_to(h, base + 2, kv.at[h, left, pl.ds(0, half)], (x + 1, y, z, core))
        kv_arrived(h, base + 1, kv.at[h, right])
        kv_send_to(h, base + 3, kv.at[h, right, pl.ds(half, half)], (x - 1, y, z, core))

    def kv_first(h):
        other = kv.at[h, x * 2 + 1 - yhi]
        kv_arrived(h, 0, other)
        kv_send_to(h, 5, other, (x + 1, y, z, core))
        kv_send_to(h, 6, other, (x - 1, y, z, core))
        spread(h, yhi, 1)

    def kv_second(h):
        spread(h, 1 - yhi, 5)

    def kv_last(h):
        far = ((x + 2) % X) * 2
        for yh, base in ((yhi, 1), (1 - yhi, 5)):
            kv_arrived(h, base + 2, kv.at[h, far + yh, pl.ds(0, half)])
            kv_arrived(h, base + 3, kv.at[h, far + yh, pl.ds(half, half)])
        out = pltpu.make_async_copy(kv.at[h], kv_ref.at[h], out_sem.at[h])
        out.start()
        outs.append(out)

    outs = []
    w_start(0)
    for n, at in enumerate(peers):
        send(codes.at[ctx], codes.at[ctx], c_send.at[n], c_recv.at[n], at)

    @pl.loop(0, tokens // 32)
    def _(n):
        part = pl.ds(pl.multiple_of(n * 32, 32), 32)
        wide = hidden_ref[part, :].astype(jnp.float32)
        scale = lax.rsqrt(jnp.mean(wide * wide, axis=-1, keepdims=True) + EPS)
        normed[part, :] = (wide * scale * gain_ref[...]).astype(jnp.bfloat16)

    w_step(0, 1); w_step(0, 2); w_step(0, 3)
    w_start(1)
    w_step(0, 4)
    w_step(1, 1)
    w_other(0)
    w_step(1, 2)
    project(0)
    w_step(1, 3)
    w_start(2)
    w_step(1, 4)
    w_step(2, 1)
    kv_first(0)
    w_other(1)
    w_step(2, 2)
    project(1)
    w_step(2, 3)
    w_start(3)
    kv_second(0)
    w_step(2, 4)
    w_step(3, 1)
    kv_first(1)
    w_other(2)
    w_step(3, 2)
    project(2)
    w_step(3, 3)
    kv_second(1)
    kv_last(0)
    w_step(3, 4)
    w_other(3)
    kv_first(2)
    project(3)
    kv_last(1)
    kv_second(2)
    kv_first(3)
    kv_last(2)
    kv_second(3)
    for n, (px, py, _, _) in enumerate(peers):
        dx, dy = [(dx, dy) for dx in range(X) for dy in (0, 2) if (dx, dy) != (0, 0)][n]
        src = ((x + X - dx) % X) * 2 + (yhi + dy // 2) % 2
        arrived(codes.at[src], c_send.at[n], c_recv.at[n])
    out = pltpu.make_async_copy(codes, codes_ref, out_sem.at[KVH])
    out.start()
    outs.append(out)
    kv_last(3)
    for copy in sent:
        copy.wait_send()
    for out in outs:
        out.wait()


def gather(hidden, norm_gain, key_gain, cos, sin, code, k_weight, v_weight):
    tokens, features = hidden.shape
    rows = k_weight.shape[0]
    vm = pl.BlockSpec(memory_space=pltpu.VMEM)
    dma = pltpu.SemaphoreType.DMA
    return pl.pallas_call(
        gather_kernel,
        out_shape=(jax.ShapeDtypeStruct((KVH, X * 2, tokens, 2 * HD), jnp.bfloat16), jax.ShapeDtypeStruct((X * 2, 1, tokens), jnp.int32)),
        in_specs=[vm] * 8,
        out_specs=(pl.BlockSpec(memory_space=pl.ANY), pl.BlockSpec(memory_space=pl.ANY)),
        scratch_shapes=[
            pltpu.VMEM((KVH, Z, 2, 2, rows, 2 * HD), jnp.bfloat16),
            pltpu.VMEM((tokens, features), jnp.bfloat16),
            pltpu.VMEM((KVH, X * 2, tokens, 2 * HD), jnp.bfloat16),
            pltpu.VMEM((X * 2, 1, tokens), jnp.int32),
            dma((KVH, 2, 4)), dma((KVH, 2, 4)), dma((KVH, 8)), dma((KVH, 8)), dma((KVH, 2)), dma((KVH, 2)),
            dma((KVH, 9)), dma((KVH, 9)), dma((7,)), dma((7,)), dma((KVH + 1,)),
        ],
        compiler_params=pltpu.CompilerParams(collective_id=0, has_side_effects=True, vmem_limit_bytes=50 * 2**20),
        cost_estimate=pl.CostEstimate(flops=3 * 10**9, bytes_accessed=10**8, transcendentals=0),
        name="project_and_gather",
    )(hidden, norm_gain, key_gain, cos, sin, code, k_weight, v_weight)


def attend_kernel(rows, q_ref, kv_ref, key_code_ref, own_code_ref, o_ref, s_ref, acc_ref, den_ref, lim_ref):
    tiles = key_code_ref.shape[0]
    slots = rows // tiles
    keys_in = GROUPS * slots
    shift = math.log2(math.e) / math.sqrt(HD)
    kc = key_code_ref[...]
    k_min = jnp.min(kc, axis=1, keepdims=True)
    k_max = jnp.max(kc, axis=1, keepdims=True)
    lim_ref[...] = jnp.concatenate([k_min, k_max] + [jnp.zeros((tiles, 126), jnp.int32)], axis=1)

    def one_tile(i, _):
        base = pl.multiple_of(i * slots, slots)
        own = own_code_ref[pl.ds(base, slots), :]
        start = (own // BIG) * BIG
        q_max = jnp.max(own)
        q_low = jnp.min(start)
        qs = []
        for k in range(KVH):
            blk = q_ref[pl.ds(base, slots), k * G * HD:(k + 1) * G * HD]
            qs.append(jnp.concatenate([blk[:, g * HD:(g + 1) * HD] for g in range(G)], axis=0))
        active = (k_min <= q_max) & (k_max >= q_low)
        where = lax.broadcasted_iota(jnp.int32, (tiles, 1), 0)
        first = jnp.min(jnp.where(active, where, tiles))
        last = jnp.max(jnp.where(active, where, -1))

        def scores(j, tops):
            codes = key_code_ref[pl.ds(j, 1), :]
            allowed = (codes <= own) & (codes >= start)
            bias = jnp.where(allowed, jnp.float32(3e38), jnp.float32(NEG))
            out = []
            for k in range(KVH):
                kt = kv_ref[k, :, pl.ds(pl.multiple_of(j * slots, slots), slots), :HD].reshape(keys_in, HD)
                s = lax.dot_general(qs[k], kt, (((1,), (1,)), ((), ())), preferred_element_type=jnp.float32)
                s = jnp.minimum(s.reshape(G, slots, keys_in), bias[None]).reshape(G * slots, keys_in)
                s_ref[k, j] = s
                out.append(jnp.maximum(tops[k], jnp.maximum(s[:, :HD], s[:, HD:])))
            return tuple(out)

        tops = lax.fori_loop(first, last + 1, scores, tuple(jnp.full((G * slots, HD), NEG, jnp.float32) for _ in range(KVH)))
        tops = [jnp.max(t, axis=1, keepdims=True) * shift for t in tops]
        acc_ref[...] = jnp.zeros_like(acc_ref)
        den_ref[...] = jnp.zeros_like(den_ref)

        def weigh(j, _):
            for k in range(KVH):
                vt = kv_ref[k, :, pl.ds(pl.multiple_of(j * slots, slots), slots), HD:].reshape(keys_in, HD)
                w = jnp.exp2(s_ref[k, j] * shift - tops[k])
                den_ref[k] += w[:, :HD] + w[:, HD:]
                acc_ref[k] += jnp.dot(w.astype(jnp.bfloat16), vt, preferred_element_type=jnp.float32)
            return 0

        lax.fori_loop(first, last + 1, weigh, 0)
        for k in range(KVH):
            total = jnp.sum(den_ref[k], axis=1, keepdims=True)
            res = (acc_ref[k] / total).astype(jnp.bfloat16)
            for g in range(G):
                o_ref[pl.ds(base, slots), (k * G + g) * HD:(k * G + g + 1) * HD] = res[g * slots:(g + 1) * slots]
        return 0

    lax.fori_loop(0, tiles, one_tile, 0)

def attend(queries, kv, key_code, own_code):
    rows = queries.shape[0]
    tiles = key_code.shape[0]
    slots = rows // tiles
    m = G * slots
    vm = pl.BlockSpec(memory_space=pltpu.VMEM)
    return pl.pallas_call(
        functools.partial(attend_kernel, rows),
        out_shape=jax.ShapeDtypeStruct(queries.shape, jnp.bfloat16),
        in_specs=[vm] * 4, out_specs=vm,
        scratch_shapes=[pltpu.VMEM((KVH, tiles, m, GROUPS * slots), jnp.float32), pltpu.VMEM((KVH, m, HD), jnp.float32),
                        pltpu.VMEM((KVH, m, HD), jnp.float32), pltpu.VMEM((tiles, 128), jnp.int32)],
        compiler_params=pltpu.CompilerParams(vmem_limit_bytes=48 * 2**20),
        cost_estimate=pl.CostEstimate(flops=10**10, bytes_accessed=10**7, transcendentals=10**7),
        name="attend",
    )(queries, kv, key_code, own_code)


def on_device(hidden, queries, norm_gain, key_gain, k_weight, v_weight, segment, position):
    tokens = hidden.shape[1]
    half = HD // 2
    freq = jnp.exp(jnp.arange(half, dtype=jnp.float32) * (-2.0 * math.log(THETA) / HD))
    angle = position[0].astype(jnp.float32)[:, None] * freq[None, :]
    cosine, sine = jnp.cos(angle), jnp.sin(angle)
    code = segment * BIG + position
    kv, codes = gather(
        hidden[0], norm_gain[None], key_gain[None], jnp.concatenate([cosine, cosine], axis=1),
        jnp.concatenate([-sine, sine], axis=1), code, k_weight, v_weight)
    tiles = 8
    key_code = codes.reshape(GROUPS, tiles, tokens // tiles).transpose(1, 0, 2).reshape(tiles, -1)
    return attend(queries[0], kv, key_code, code.reshape(tokens, 1))[None]


def solution(mesh):
    placed = (
        P("fsdp", "ctx", None),
        P("fsdp", "ctx", None),
        P(),
        P(),
        P("fsdp", None),
        P("fsdp", None),
        P("fsdp", "ctx"),
        P("fsdp", "ctx"),
    )
    return jax.shard_map(
        on_device, mesh=mesh, in_specs=placed, out_specs=P("fsdp", "ctx", None), check_vma=False
    )
```

time: 314 us -> 125 us (0.40)
  the two profiles are of different devices: /device:TPU:1 before, /device:TPU:224 now
where the time goes in v1:
time: 125 us
  Pallas kernels  118 us (94%)
  local copies, waits for them, and re-layouts  5.24 us (4%)
  other arithmetic  1.47 us (1%)
    pallas_call x1, Pallas kernels, gather(): pl.pallas_call(gather_kernel, out_shape=(jax.ShapeDtypeStruct((KVH, X * 2...  82.4 us
    pallas_call x1, Pallas kernels, attend(): pl.pallas_call(functools.partial(attend_kernel, rows), out_shape=jax.Shap...  35.4 us
    unnamed x12, local copies, waits for them, and re-layouts  4.95 us

profile of v1, /device:TPU:224, one launch (start us, length us, event | category | flops | bytes accessed | tf_op | source)
XLA Modules:
  0.0 124.5 jit_solution(7896685820986689289)
XLA Ops:
  0.0 0.8 multiply_add_fusion
  0.8 0.1 copy.11.own_code_ref
  0.9 0.5 fusion
  1.5 0.1 pad_maximum_fusion
  1.6 0.0 copy-start
  1.6 1.7 %copy-done = bf16[1,256,5120]{2,1,0:T(8,128)(2,1)S(1)} copy-done((bf16[1,256,5120]{2,1,0:T(8,128)(2,1)S(1)}, bf16[1,256,5120]{2,1,0:T(8,128)(2,1)}, u32[]{:S(2)}) %copy-start) | copy-done | bytes 2621464
  3.3 0.0 copy-start.2
  3.4 0.9 copy-done.2
  4.3 0.0 copy-start.3
  4.3 0.9 copy-done.3
  5.2 0.0 copy-start.4
  5.2 0.7 copy-done.4
  5.9 0.0 copy-start.5
  5.9 0.7 copy-done.5
  6.6 0.0 copy-start.1
  6.6 82.4 %project_and_gather.1 = (bf16[4,8,256,256]{3,2,1,0:T(8,128)(2,1)}, s32[8,1,256]{2,1,0:T(1,128)S(1)}) custom-call(bf16[256,5120]{1,0:T(8,128)(2,1)S(1)} %bitcast.11, f32[1,5120]{1,0:T(1,128)S(1)} %bitcast.13, f32[1,128]{1,0:T(1,128)S(1)} %bitcast.14, f32[256,128]{1,0:T(8,128)S(1)} %get-tuple-element.14.cos_ref, f32[256,128]{1,0:T(8,128)S(1)} %get-tuple-element.15.sin_ref, ...), custom_call_target="tpu_custom_call" | custom-call | flops 3000000000 | bytes 100000000 | tf_op jit(solution)/shard_map/project_and_gather/pallas_call | solution.py:225
  89.0 0.1 reshape.20
  89.1 0.1 reshape.21.key_code_ref
  89.2 0.0 copy-done.1
  89.2 35.4 %attend.1 = bf16[256,4096]{1,0:T(8,128)(2,1)} custom-call(bf16[256,4096]{1,0:T(8,128)(2,1)S(1)} %bitcast.12, bf16[4,8,256,256]{3,2,1,0:T(8,128)(2,1)} %get-tuple-element.7.kv_ref, s32[8,256]{1,0:T(8,128)S(1)} %reshape.21.key_code_ref, s32[256,1]{1,0:T(8,128)S(1)} %copy.11.own_code_ref), custom_call_target="tpu_custom_call" | custom-call | flops 10000000000 | bytes 10000000 | tf_op jit(solution)/shard_map/attend/pallas_call | solution.py:311
  (3 shorter events, 0.0 us)
Async XLA Ops:
  1.6 1.7 %copy-start = (bf16[1,256,5120]{2,1,0:T(8,128)(2,1)S(1)}, bf16[1,256,5120]{2,1,0:T(8,128)(2,1)}, u32[]{:S(2)}) copy-start(bf16[1,256,5120]{2,1,0:T(8,128)(2,1)} %param.8) | copy-start | bytes 7864324
  3.3 0.9 copy-start.2
  4.3 0.9 copy-start.3
  5.2 0.7 copy-start.4
  5.9 0.7 copy-start.5
  6.6 82.6 %copy-start.1 = (bf16[1,256,4096]{2,1,0:T(8,128)(2,1)S(1)}, bf16[1,256,4096]{2,1,0:T(8,128)(2,1)}, u32[]{:S(2)}) copy-start(bf16[1,256,4096]{2,1,0:T(8,128)(2,1)} %param.9) | copy-start | bytes 6291460

commit v2 on v0

v2 whole, which is shorter than its diff:
```python
import functools
import math

import jax
import jax.numpy as jnp
from jax import lax
from jax.experimental import pallas as pl
from jax.experimental.pallas import tpu as pltpu
from jax.sharding import PartitionSpec as P

KVH = 4
HD = 128
G = 8
GROUPS = 8
EPS = 1e-06
THETA = 1000000.0
BIG = 8192
NEG = -1e30
X, Y, Z = 4, 4, 8
TILES = 4
MESH = pl.DeviceIdType.MESH


def place():
    f = lax.axis_index("fsdp")
    c = lax.axis_index("ctx")
    return c // 2, (c % 2) * 2 + (f // 2) % 2, f // 4, f % 2


def device(x, y, z, core):
    x, y, z = (x + X) % X, (y + Y) % Y, (z + Z) % Z
    return {"fsdp": (z * 2 + y % 2) * 2 + core, "ctx": x * 2 + y // 2}


ORDER = (
    "z000", "z300", "z310", "r", "h0", "z010", "z001", "z210", "z301", "m", "z011", "z100", "z211", "z002", "z012",
    "h1", "z302", "h3", "z200", "z311", "z013", "z003", "n", "z303", "z312", "z101", "z201", "z004", "z110", "E0",
    "z304", "z212", "z313", "h2", "o0", "o3", "E3", "f0", "z102", "z202", "p0", "f3", "z111", "z213", "z103", "p3",
    "z203", "K00", "o2", "z112", "L0", "o1", "K01", "z204", "z104", "z113", "K30", "K31", "E2", "f2", "q", "M00",
    "E1", "M01", "L3", "Q0", "f1", "p2", "Q3", "p1", "N0", "A00", "A01", "K20", "K21", "A02", "M31", "M30", "L2",
    "A03", "N3", "A30", "Q2", "K11", "K10", "A31", "A32", "A33", "L1", "Q1", "M20", "M21", "N2", "A20", "A21",
    "A22", "A23", "M10", "M11", "N1", "A10", "A11", "A12", "A13",
)
BY_Y = (0, 1, 2, 3)
ALL_Y = (0,)


def fused_kernel(
    hidden_hbm, queries_hbm, gain_hbm, key_gain_hbm, segment_hbm, position_hbm, kw_hbm, vw_hbm,
    out_hbm,
    hidden, queries, gain_ref, key_gain_ref, segment_ref, position_ref, kw, vw, wbuf, normed, kv, codes, perm, perm_t, cos, sin, own_code, bias, held, rows_out, out,
    in_sem, z_send, z_recv, o_send, o_recv, h_send, h_recv, y_send, y_recv, d_send, d_recv,
    kv_send, kv_recv, c_send, c_recv, out_sem,
):
    x, y, z, core = place()
    ylo, yhi = y % 2, y // 2
    ctx = x * 2 + yhi
    sgn = 1 - 2 * core
    rows = kw.shape[0]
    width = 2 * HD
    tokens = hidden.shape[0]
    half = tokens // 2
    slots = tokens // TILES
    m, keys_in = G * slots, GROUPS * slots
    shift = math.log2(math.e) / math.sqrt(HD)

    loads = [pltpu.make_async_copy(a, b, in_sem.at[n]) for n, (a, b) in enumerate(((kw_hbm, kw), (vw_hbm, vw), (segment_hbm, segment_ref), (position_hbm, position_ref), (key_gain_hbm, key_gain_ref), (gain_hbm, gain_ref), (hidden_hbm, hidden), (queries_hbm, queries)))]
    for load in loads:
        load.start()
    peers = [(x + dx, y + dy, z, core) for dx in range(X) for dy in (0, 2) if (dx, dy) != (0, 0)]
    near = [(x, y, z + 1, core), (x, y, z - 1, core), (x, y + 1, z, core), (x, y - 1, z, core), (x, y, z, 1 - core)]
    barrier = pltpu.get_barrier_semaphore()
    for at in near + peers:
        pl.semaphore_signal(barrier, inc=1, device_id=device(*at), device_id_type=MESH)
    loads[0].wait()
    loads[1].wait()
    for h in range(KVH):
        wbuf[h, z, ylo, core, :, :HD] = kw[:, h * HD:(h + 1) * HD]
        wbuf[h, z, ylo, core, :, HD:] = vw[:, h * HD:(h + 1) * HD]
    pl.semaphore_wait(barrier, len(peers + near))

    sent = []
    outs = []

    def send(src, dst, ssem, rsem, at):
        copy = pltpu.make_async_remote_copy(
            src_ref=src, dst_ref=dst, send_sem=ssem, recv_sem=rsem, device_id=device(*at), device_id_type=MESH)
        copy.start()
        sent.append(copy)

    def arrived(dst, ssem, rsem):
        pltpu.make_async_remote_copy(
            src_ref=dst, dst_ref=dst, send_sem=ssem, recv_sem=rsem, device_id=device(x, y, z, 1 - core),
            device_id_type=MESH).wait_recv()

    def slab(h, zz, yl):
        return wbuf.at[h, (zz + 2 * Z) % Z, yl, core]

    def ring(h, way, step):
        way_z = -sgn if way == 0 else sgn
        block = slab(h, z + way_z * step, ylo)
        if step > 0:
            arrived(block, z_send.at[h, way, step - 1], z_recv.at[h, way, step - 1])
        if step < (4 if way == 0 else 3):
            send(block, block, z_send.at[h, way, step], z_recv.at[h, way, step], (x, y, z - way_z, core))
        if step > (0 if h in ALL_Y else 1):
            send(block, block, y_send.at[h, way, step - 1], y_recv.at[h, way, step - 1], (x, y - way_z, z, core))

    def halves(h, zz, yl):
        block = slab(h, zz, yl)
        return block.at[pl.ds(0, rows // 2)], block.at[pl.ds(rows // 2, rows // 2)]

    def cross(h):
        low, high = halves(h, z, ylo)
        send(low, low, h_send.at[h, 0], h_recv.at[h, 0], (x, y + 1, z, core))
        send(high, high, h_send.at[h, 1], h_recv.at[h, 1], (x, y - 1, z, core))

    def crossed(h):
        low, high = halves(h, z, 1 - ylo)
        arrived(low, h_send.at[h, 0], h_recv.at[h, 0])
        arrived(high, h_send.at[h, 1], h_recv.at[h, 1])
        if h not in ALL_Y:
            block = slab(h, z, 1 - ylo)
            send(block, block, o_send.at[h, 0], o_recv.at[h, 0], (x, y, z + 1, core))
            send(block, block, o_send.at[h, 1], o_recv.at[h, 1], (x, y, z - 1, core))

    def share_own(h):
        own = wbuf.at[h, :, ylo, core]
        send(own, own, d_send.at[h, 0], d_recv.at[h, 0], (x, y, z, 1 - core))

    def share_other(h):
        if h not in ALL_Y:
            arrived(slab(h, z - 1, 1 - ylo), o_send.at[h, 0], o_recv.at[h, 0])
            arrived(slab(h, z + 1, 1 - ylo), o_send.at[h, 1], o_recv.at[h, 1])
        for way in (0, 1):
            way_z = -sgn if way == 0 else sgn
            for k in range(0 if h in ALL_Y else 1, 4 - way):
                arrived(slab(h, z + way_z * (k + 1), 1 - ylo), y_send.at[h, way, k], y_recv.at[h, way, k])
        own = wbuf.at[h, :, 1 - ylo, core]
        send(own, own, d_send.at[h, 1], d_recv.at[h, 1], (x, y, z, 1 - core))

    def kv_send_to(h, n, block, at):
        send(block, block, kv_send.at[h, n], kv_recv.at[h, n], at)

    def kv_arrived(h, n, block):
        arrived(block, kv_send.at[h, n], kv_recv.at[h, n])

    def project(h):
        arrived(wbuf.at[h, :, ylo, 1 - core], d_send.at[h, 0], d_recv.at[h, 0])
        arrived(wbuf.at[h, :, 1 - ylo, 1 - core], d_send.at[h, 1], d_recv.at[h, 1])
        sums = jnp.zeros((tokens, width), jnp.float32)
        deep = 4 * rows
        for n in range(Z):
            sums += jnp.dot(normed[:, n * deep:(n + 1) * deep], wbuf[h, n].reshape(deep, width), preferred_element_type=jnp.float32)
        raw = sums[:, :HD]
        normk = raw * lax.rsqrt(jnp.mean(raw * raw, axis=-1, keepdims=True) + EPS) * key_gain_ref[...]
        turned = jnp.concatenate([normk[:, HD // 2:], normk[:, :HD // 2]], axis=1)
        keys = (normk * cos[...] + turned * sin[...]).astype(jnp.bfloat16)
        both = jnp.concatenate([keys, sums[:, HD:].astype(jnp.bfloat16)], axis=1)
        kv[h, ctx] = jnp.dot(perm[...], both, preferred_element_type=jnp.float32).astype(jnp.bfloat16)
        block = kv.at[h, ctx]
        kv_send_to(h, 0, block, (x, y + 2, z, core))
        kv_send_to(h, 1, block, (x + 1, y, z, core))
        kv_send_to(h, 2, block, (x - 1, y, z, core))

    def spread(h, yh, base, side):
        step = 1 if side == 0 else -1
        block = kv.at[h, ((x - step + X) % X) * 2 + yh]
        kv_arrived(h, base + side, block)
        if base == 1 or h not in BY_Y:
            part = block.at[pl.ds(side * half, half)]
            kv_send_to(h, base + 2 + side, part, (x + step, y, z, core))

    def kv_partner(h):
        other = kv.at[h, x * 2 + 1 - yhi]
        kv_arrived(h, 0, other)
        kv_send_to(h, 5, other, (x + 1, y, z, core))
        kv_send_to(h, 6, other, (x - 1, y, z, core))

    def far(h, yh):
        return kv.at[h, ((x + 2) % X) * 2 + yh]

    def kv_far(h):
        for side in (0, 1):
            kv_arrived(h, 3 + side, far(h, yhi).at[pl.ds(side * half, half)])
        if h in BY_Y:
            kv_send_to(h, 9, far(h, yhi), (x, y + 2, z, core))

    def kv_last(h):
        if h in BY_Y:
            kv_arrived(h, 9, far(h, 1 - yhi))
        else:
            for side in (0, 1):
                kv_arrived(h, 7 + side, far(h, 1 - yhi).at[pl.ds(side * half, half)])

    def order():
        shape = (tokens, tokens)
        down, across = lax.broadcasted_iota(jnp.int32, shape, 0), lax.broadcasted_iota(jnp.int32, shape, 1)
        same = down == across

        def column(row):
            return jnp.sum(jnp.where(same, row, 0.0), axis=1, keepdims=True)

        for load in loads[2:5]:
            load.wait()
        where = position_ref[...].astype(jnp.float32)
        row = (segment_ref[...] * BIG + position_ref[...]).astype(jnp.float32)
        col = column(row)
        rank_row = jnp.sum(jnp.where(col < row, 1.0, 0.0), axis=0, keepdims=True)
        rank_col = jnp.sum(jnp.where(row < col, 1.0, 0.0), axis=1, keepdims=True)
        put = rank_row == down.astype(jnp.float32)
        take = rank_col == across.astype(jnp.float32)
        perm[...] = jnp.where(put, 1.0, 0.0).astype(jnp.bfloat16)
        perm_t[...] = jnp.where(take, 1.0, 0.0).astype(jnp.bfloat16)
        codes[ctx] = jnp.sum(jnp.where(take, col, 0.0), axis=0, keepdims=True).astype(jnp.int32)
        own_code[...] = jnp.broadcast_to(jnp.sum(jnp.where(put, row, 0.0), axis=1, keepdims=True), (tokens, HD)).astype(jnp.int32)
        for n, at in enumerate(peers):
            send(codes.at[ctx], codes.at[ctx], c_send.at[n], c_recv.at[n], at)
        lane = lax.broadcasted_iota(jnp.int32, (1, HD), 1)
        freq = jnp.exp((lane % (HD // 2)).astype(jnp.float32) * (-2.0 * math.log(THETA) / HD))
        angle = column(where) * freq
        cos[...] = jnp.cos(angle)
        sin[...] = jnp.where(lane < HD // 2, -1.0, 1.0) * jnp.sin(angle)

    def masks():
        for n in range(len(peers)):
            dx, dy = [(dx, dy) for dx in range(X) for dy in (0, 2) if (dx, dy) != (0, 0)][n]
            src = ((x + X - dx) % X) * 2 + (yhi + dy // 2) % 2
            arrived(codes.at[src], c_send.at[n], c_recv.at[n])
        own = own_code[:, :1]
        start = own // BIG * BIG
        for j in range(TILES):
            there = jnp.concatenate([codes[d, :, j * slots:(j + 1) * slots] for d in range(GROUPS)], axis=1)
            bias[j] = jnp.where((there <= own) & (there >= start), jnp.float32(3e38), jnp.float32(NEG))

    def sort_queries():
        loads[7].wait()
        for h in range(KVH):
            part = pl.ds(h * G * HD, G * HD)
            queries[:, part] = jnp.dot(perm[...], queries[:, part], preferred_element_type=jnp.float32).astype(jnp.bfloat16)

    def attend(h, i):
        blk = queries[i * slots:(i + 1) * slots, h * G * HD:(h + 1) * G * HD]
        q = jnp.concatenate([blk[:, g * HD:(g + 1) * HD] for g in range(G)], axis=0)

        def tiles(lanes):
            parts = [kv[h, :, j * slots:(j + 1) * slots, lanes].reshape(keys_in, HD) for j in range(i + 1)]
            return jnp.concatenate(parts, axis=0)

        s = lax.dot_general(q, tiles(slice(0, HD)), (((1,), (1,)), ((), ())), preferred_element_type=jnp.float32)
        top = None
        for j in range(i + 1):
            t = s[:, j * keys_in:(j + 1) * keys_in].reshape(G, slots, keys_in)
            t = jnp.minimum(t, bias[j, i * slots:(i + 1) * slots, :][None]).reshape(m, keys_in)
            held[j] = t
            most = jnp.maximum(jnp.maximum(t[:, :HD], t[:, HD:2 * HD]), jnp.maximum(t[:, 2 * HD:3 * HD], t[:, 3 * HD:]))
            top = most if top is None else jnp.maximum(top, most)
        low = jnp.max(top, axis=1, keepdims=True) * shift
        w = jnp.concatenate([jnp.exp2(held[j] * shift - low).astype(jnp.bfloat16) for j in range(i + 1)], axis=1)
        value = tiles(slice(HD, 2 * HD))
        acc = jnp.dot(w, jnp.concatenate([value, jnp.ones_like(value)], axis=1), preferred_element_type=jnp.float32)
        res = (acc[:, :HD] / acc[:, HD:]).astype(jnp.bfloat16)
        part = pl.ds(i * slots, slots)
        rows_out[part, :] = jnp.concatenate([res[g * slots:(g + 1) * slots] for g in range(G)], axis=1)
        if i == TILES - 1:
            out[h] = jnp.dot(perm_t[...], rows_out[...], preferred_element_type=jnp.float32).astype(jnp.bfloat16)
            copy = pltpu.make_async_copy(out.at[h], out_hbm.at[:, pl.ds(h * G * HD, G * HD)], out_sem.at[h])
            copy.start()
            outs.append(copy)

    def norm():
        loads[5].wait()
        loads[6].wait()

        @pl.loop(0, tokens // 32)
        def _(n):
            part = pl.ds(pl.multiple_of(n * 32, 32), 32)
            wide = hidden[part, :].astype(jnp.float32)
            scale = lax.rsqrt(jnp.mean(wide * wide, axis=-1, keepdims=True) + EPS)
            normed[part, :] = (wide * scale * gain_ref[...]).astype(jnp.bfloat16)

    steps = {
        "z": ring, "h": cross, "o": crossed, "E": share_own, "f": share_other, "p": project,
        "K": lambda h, side: spread(h, yhi, 1, side), "L": kv_partner,
        "M": lambda h, side: spread(h, 1 - yhi, 5, side), "Q": kv_far, "N": kv_last, "A": attend,
    }
    plain = {"n": norm, "r": order, "m": masks, "q": sort_queries}
    for item in ORDER:
        if item in plain:
            plain[item]()
        else:
            steps[item[0]](*[int(digit) for digit in item[1:]])
    for copy in sent:
        copy.wait_send()
    for out in outs:
        out.wait()


def fused(hidden, queries, norm_gain, key_gain, segment, position, k_weight, v_weight):
    tokens, features = hidden.shape
    rows = k_weight.shape[0]
    slots = tokens // TILES
    m, keys_in = G * slots, GROUPS * slots
    hbm = pl.BlockSpec(memory_space=pl.ANY)
    dma = pltpu.SemaphoreType.DMA
    half, full = jnp.bfloat16, jnp.float32
    return pl.pallas_call(
        fused_kernel,
        out_shape=jax.ShapeDtypeStruct(queries.shape, half),
        in_specs=[hbm] * 8,
        out_specs=hbm,
        scratch_shapes=[
            pltpu.VMEM((tokens, features), half),
            pltpu.VMEM(queries.shape, half),
            pltpu.VMEM(norm_gain.shape, full),
            pltpu.VMEM(key_gain.shape, full),
            pltpu.VMEM(segment.shape, jnp.int32),
            pltpu.VMEM(position.shape, jnp.int32),
            pltpu.VMEM(k_weight.shape, half),
            pltpu.VMEM(v_weight.shape, half),
            pltpu.VMEM((KVH, Z, 2, 2, rows, 2 * HD), half),
            pltpu.VMEM((tokens, features), half),
            pltpu.VMEM((KVH, GROUPS, tokens, 2 * HD), half),
            pltpu.VMEM((GROUPS, 1, tokens), jnp.int32),
            pltpu.VMEM((tokens, tokens), half),
            pltpu.VMEM((tokens, tokens), half),
            pltpu.VMEM((tokens, HD), full),
            pltpu.VMEM((tokens, HD), full),
            pltpu.VMEM((tokens, HD), jnp.int32),
            pltpu.VMEM((TILES, tokens, keys_in), full),
            pltpu.VMEM((TILES, m, keys_in), full),
            pltpu.VMEM((tokens, G * HD), half),
            pltpu.VMEM((KVH, tokens, G * HD), half),
            dma((8,)),
            dma((KVH, 2, 4)), dma((KVH, 2, 4)), dma((KVH, 2)), dma((KVH, 2)), dma((KVH, 2)), dma((KVH, 2)),
            dma((KVH, 2, 4)), dma((KVH, 2, 4)), dma((KVH, 2)), dma((KVH, 2)),
            dma((KVH, 10)), dma((KVH, 10)), dma((7,)), dma((7,)), dma((KVH,)),
        ],
        compiler_params=pltpu.CompilerParams(collective_id=0, has_side_effects=True, vmem_limit_bytes=60 * 2**20),
        cost_estimate=pl.CostEstimate(flops=12 * 10**9, bytes_accessed=10**8, transcendentals=2 * 10**7),
        name="project_gather_attend",
    )(hidden, queries, norm_gain, key_gain, segment, position, k_weight, v_weight)


def on_device(hidden, queries, norm_gain, key_gain, k_weight, v_weight, segment, position):
    return fused(hidden[0], queries[0], norm_gain[None], key_gain[None], segment, position, k_weight, v_weight)[None]


def solution(mesh):
    placed = (
        P("fsdp", "ctx", None),
        P("fsdp", "ctx", None),
        P(),
        P(),
        P("fsdp", None),
        P("fsdp", None),
        P("fsdp", "ctx"),
        P("fsdp", "ctx"),
    )
    return jax.shard_map(
        on_device, mesh=mesh, in_specs=placed, out_specs=P("fsdp", "ctx", None), check_vma=False
    )
```

time: 314 us -> 86.3 us (0.27)
  waiting for transfers between devices: 164 us -> 0 us
  Pallas kernels: 0 us -> 83.1 us
  matrix products: 62 us -> 0 us
  blocking collectives: 34.1 us -> 0 us
  other arithmetic: 27.7 us -> 0 us
  between operations: 13.2 us -> 0.01 us
  local copies, waits for them, and re-layouts: 13.1 us -> 3.13 us
    all_gather x4 -> x0, waiting for transfers between devices: 162 us -> none  [the longest x1 70.2 us: on_device(): lax.all_gather(k_weight, 'fsdp', axis=0, tiled=True)]
    pallas_call x0 -> x1, Pallas kernels: none -> 83.1 us  [fused(): pl.pallas_call(fused_kernel, out_shape=jax.ShapeDtypeStruct(queries.shape...]
    dot_general x4 -> x0, matrix products: 62 us -> none  [the longest x1 26 us: on_device(): jnp.einsum('tkgd,skd->kgts', grouped, key_piece[0], preferred_element_typ...]
    all_gather x2 -> x0, blocking collectives: 34.1 us -> none  [the longest x1 19.3 us: on_device(): pos_piece = lax.all_gather(position, 'ctx', axis=1, tiled=True)]
    reduce_sum x2 -> x0, other arithmetic: 24.3 us -> none  [the longest x1 22 us: on_device(): total = jnp.sum(weights, axis=-1)]
    dot_general x1 -> x0, local copies, waits for them, and re-layouts: 8.12 us -> none  [on_device(): jnp.dot(normed, lax.all_gather(k_weight, 'fsdp', axis=0, tiled=True), pre...]
  transfers between devices with their start and end apart: 4 -> 0, of which waited for: 4 -> 0; matrix products, arithmetic and copies ran while one was open for 24% -> 0% of each run, Pallas kernels for 0% -> 0%
where the time goes in v2:
time: 86.3 us; the launch traced here: 86.2 us
  Pallas kernels  83.1 us (96%)
  local copies, waits for them, and re-layouts  3.13 us (4%)
    pallas_call x1, Pallas kernels, fused(): pl.pallas_call(fused_kernel, out_shape=jax.ShapeDtypeStruct(queries.shape...  83.1 us
    unnamed x1, local copies, waits for them, and re-layouts  3.13 us

profile of v2, /device:TPU:1, one launch (start us, length us, event | category | flops | bytes accessed | tf_op | source)
XLA Modules:
  0.0 86.2 jit_solution(2756854144632049120)
XLA Ops:
  0.0 83.1 %project_gather_attend.1 = bf16[256,4096]{1,0:T(8,128)(2,1)} custom-call(bf16[256,5120]{1,0:T(8,128)(2,1)} %bitcast.6, bf16[256,4096]{1,0:T(8,128)(2,1)} %bitcast.7, f32[1,5120]{1,0:T(1,128)} %bitcast.8, f32[1,128]{1,0:T(1,128)} %bitcast.9, s32[1,256]{1,0:T(1,128)} %segment_hbm.1, s32[1,256]{1,0:T(1,128)} %position_hbm.1, bf16[160,512]{1,0:T(8,128)(2,1)} %kw_hbm.1, ...), custom_call_target="tpu_custom_call" | custom-call | flops 12000000000 | bytes 100000000 | tf_op jit(solution)/shard_map/project_gather_attend/pallas_call | solution.py:307
  83.1 3.1 %copy.10 = bf16[1,256,4096]{2,1,0:T(8,128)(2,1)} copy(bf16[1,256,4096]{2,1,0:T(8,128)(2,1)} %bitcast.5) | data formatting | bytes 4194304

commit v3 on v2

--- a/solution.py
+++ b/solution.py
@@ -33,22 +33,26 @@
 
 
 ORDER = (
-    "z000", "z300", "z310", "r", "h0", "z010", "z001", "z210", "z301", "m", "z011", "z100", "z211", "z002", "z012",
-    "h1", "z302", "h3", "z200", "z311", "z013", "z003", "n", "z303", "z312", "z101", "z201", "z004", "z110", "E0",
-    "z304", "z212", "z313", "h2", "o0", "o3", "E3", "f0", "z102", "z202", "p0", "f3", "z111", "z213", "z103", "p3",
-    "z203", "K00", "o2", "z112", "L0", "o1", "K01", "z204", "z104", "z113", "K30", "K31", "E2", "f2", "q", "M00",
-    "E1", "M01", "L3", "Q0", "f1", "p2", "Q3", "p1", "N0", "A00", "A01", "K20", "K21", "A02", "M31", "M30", "L2",
-    "A03", "N3", "A30", "Q2", "K11", "K10", "A31", "A32", "A33", "L1", "Q1", "M20", "M21", "N2", "A20", "A21",
-    "A22", "A23", "M10", "M11", "N1", "A10", "A11", "A12", "A13",
+    "z100", "z110", "z200", "z210", "h2", "z000", "h1", "h4", "z010", "h0", "z310", "z101", "o1", "z201", "h3",
+    "z111", "z001", "r", "z102", "z211", "q", "z410", "z011", "o0", "z300", "z002", "z112", "z103", "z202", "z212",
+    "m", "n", "z012", "z104", "z113", "z003", "z301", "z203", "z013", "z400", "E1", "z411", "z311", "f1", "z004",
+    "z213", "z302", "E0", "z412", "p1", "z312", "f0", "z401", "z204", "o2", "p0", "z303", "o4", "z313", "E2", "o3",
+    "L1", "f2", "z413", "K11", "K00", "z304", "K10", "K01", "z402", "E3", "p2", "M10", "M11", "z403", "f3", "Q0",
+    "Q1", "L0", "K21", "z404", "K20", "p3", "M00", "L2", "M01", "Q2", "E4", "N0", "S00", "S01", "S02", "S03", "N1",
+    "V00", "f4", "V01", "K31", "K30", "S11", "S10", "p4", "V02", "V03", "M20", "M21", "L3", "Q3", "S13", "N2",
+    "V10", "K40", "K41", "V11", "S12", "S20", "V12", "V13", "S21", "L4", "M31", "S23", "M30", "Q4", "N3", "V20",
+    "V21", "S22", "V22", "S31", "V23", "M40", "S32", "M41", "S30", "N4", "S33", "V30", "V31", "V32", "V33",
 )
-BY_Y = (0, 1, 2, 3)
-ALL_Y = (0,)
+PARTS = KVH + 1
+BY_Y = (0, 1, 2, 3, 4)
+ALL_Y = (0, 1, 2)
 
 
 def fused_kernel(
     hidden_hbm, queries_hbm, gain_hbm, key_gain_hbm, segment_hbm, position_hbm, kw_hbm, vw_hbm,
     out_hbm,
-    hidden, queries, gain_ref, key_gain_ref, segment_ref, position_ref, kw, vw, wbuf, normed, kv, codes, perm, perm_t, cos, sin, own_code, bias, held, rows_out, out,
+    hidden, queries, gain_ref, key_gain_ref, segment_ref, position_ref, kw, vw, w_edge, w_mid, normed, kv_edge, kv_mid,
+    codes, perm, perm_t, cos, sin, own_code, bias, held, tops, rows_out, out,
     in_sem, z_send, z_recv, o_send, o_recv, h_send, h_recv, y_send, y_recv, d_send, d_recv,
     kv_send, kv_recv, c_send, c_recv, out_sem,
 ):
@@ -57,7 +61,8 @@
     ctx = x * 2 + yhi
     sgn = 1 - 2 * core
     rows = kw.shape[0]
-    width = 2 * HD
+    wbuf = [w_edge.at[0]] + [w_mid.at[n] for n in range(KVH - 1)] + [w_edge.at[1]]
+    kv = [kv_edge.at[0]] + [kv_mid.at[n] for n in range(KVH - 1)] + [kv_edge.at[1]]
     tokens = hidden.shape[0]
     half = tokens // 2
     slots = tokens // TILES
@@ -74,9 +79,12 @@
         pl.semaphore_signal(barrier, inc=1, device_id=device(*at), device_id_type=MESH)
     loads[0].wait()
     loads[1].wait()
-    for h in range(KVH):
-        wbuf[h, z, ylo, core, :, :HD] = kw[:, h * HD:(h + 1) * HD]
-        wbuf[h, z, ylo, core, :, HD:] = vw[:, h * HD:(h + 1) * HD]
+    for h in range(PARTS):
+        if h > 0:
+            wbuf[h][z, ylo, core, :, :HD] = vw[:, (h - 1) * HD:h * HD]
+        if h < KVH:
+            lanes = slice(0, HD) if h == 0 else slice(HD, 2 * HD)
+            wbuf[h][z, ylo, core, :, lanes] = kw[:, h * HD:(h + 1) * HD]
     pl.semaphore_wait(barrier, len(peers + near))
 
     sent = []
@@ -94,7 +102,7 @@
             device_id_type=MESH).wait_recv()
 
     def slab(h, zz, yl):
-        return wbuf.at[h, (zz + 2 * Z) % Z, yl, core]
+        return wbuf[h].at[(zz + 2 * Z) % Z, yl, core]
 
     def ring(h, way, step):
         way_z = -sgn if way == 0 else sgn
@@ -125,7 +133,7 @@
             send(block, block, o_send.at[h, 1], o_recv.at[h, 1], (x, y, z - 1, core))
 
     def share_own(h):
-        own = wbuf.at[h, :, ylo, core]
+        own = wbuf[h].at[:, ylo, core]
         send(own, own, d_send.at[h, 0], d_recv.at[h, 0], (x, y, z, 1 - core))
 
     def share_other(h):
@@ -136,7 +144,7 @@
             way_z = -sgn if way == 0 else sgn
             for k in range(0 if h in ALL_Y else 1, 4 - way):
                 arrived(slab(h, z + way_z * (k + 1), 1 - ylo), y_send.at[h, way, k], y_recv.at[h, way, k])
-        own = wbuf.at[h, :, 1 - ylo, core]
+        own = wbuf[h].at[:, 1 - ylo, core]
         send(own, own, d_send.at[h, 1], d_recv.at[h, 1], (x, y, z, 1 - core))
 
     def kv_send_to(h, n, block, at):
@@ -146,39 +154,42 @@
         arrived(block, kv_send.at[h, n], kv_recv.at[h, n])
 
     def project(h):
-        arrived(wbuf.at[h, :, ylo, 1 - core], d_send.at[h, 0], d_recv.at[h, 0])
-        arrived(wbuf.at[h, :, 1 - ylo, 1 - core], d_send.at[h, 1], d_recv.at[h, 1])
-        sums = jnp.zeros((tokens, width), jnp.float32)
-        deep = 4 * rows
-        for n in range(Z):
-            sums += jnp.dot(normed[:, n * deep:(n + 1) * deep], wbuf[h, n].reshape(deep, width), preferred_element_type=jnp.float32)
-        raw = sums[:, :HD]
-        normk = raw * lax.rsqrt(jnp.mean(raw * raw, axis=-1, keepdims=True) + EPS) * key_gain_ref[...]
-        turned = jnp.concatenate([normk[:, HD // 2:], normk[:, :HD // 2]], axis=1)
-        keys = (normk * cos[...] + turned * sin[...]).astype(jnp.bfloat16)
-        both = jnp.concatenate([keys, sums[:, HD:].astype(jnp.bfloat16)], axis=1)
-        kv[h, ctx] = jnp.dot(perm[...], both, preferred_element_type=jnp.float32).astype(jnp.bfloat16)
-        block = kv.at[h, ctx]
+        arrived(wbuf[h].at[:, ylo, 1 - core], d_send.at[h, 0], d_recv.at[h, 0])
+        arrived(wbuf[h].at[:, 1 - ylo, 1 - core], d_send.at[h, 1], d_recv.at[h, 1])
+        width = wbuf[h].shape[-1]
+        weight = wbuf[h][...].reshape(normed.shape[1], width)
+        sums = jnp.dot(normed[...], weight, preferred_element_type=jnp.float32)
+        made = []
+        if h > 0:
+            made.append(sums[:, :HD].astype(jnp.bfloat16))
+        if h < KVH:
+            raw = sums[:, width - HD:]
+            normk = raw * lax.rsqrt(jnp.mean(raw * raw, axis=-1, keepdims=True) + EPS) * key_gain_ref[...]
+            turned = jnp.concatenate([normk[:, HD // 2:], normk[:, :HD // 2]], axis=1)
+            made.append((normk * cos[...] + turned * sin[...]).astype(jnp.bfloat16))
+        both = jnp.concatenate(made, axis=1)
+        kv[h][ctx] = jnp.dot(perm[...], both, preferred_element_type=jnp.float32).astype(jnp.bfloat16)
+        block = kv[h].at[ctx]
         kv_send_to(h, 0, block, (x, y + 2, z, core))
         kv_send_to(h, 1, block, (x + 1, y, z, core))
         kv_send_to(h, 2, block, (x - 1, y, z, core))
 
     def spread(h, yh, base, side):
         step = 1 if side == 0 else -1
-        block = kv.at[h, ((x - step + X) % X) * 2 + yh]
+        block = kv[h].at[((x - step + X) % X) * 2 + yh]
         kv_arrived(h, base + side, block)
         if base == 1 or h not in BY_Y:
             part = block.at[pl.ds(side * half, half)]
             kv_send_to(h, base + 2 + side, part, (x + step, y, z, core))
 
     def kv_partner(h):
-        other = kv.at[h, x * 2 + 1 - yhi]
+        other = kv[h].at[x * 2 + 1 - yhi]
         kv_arrived(h, 0, other)
         kv_send_to(h, 5, other, (x + 1, y, z, core))
         kv_send_to(h, 6, other, (x - 1, y, z, core))
 
     def far(h, yh):
-        return kv.at[h, ((x + 2) % X) * 2 + yh]
+        return kv[h].at[((x + 2) % X) * 2 + yh]
 
     def kv_far(h):
         for side in (0, 1):
@@ -239,26 +250,33 @@
             part = pl.ds(h * G * HD, G * HD)
             queries[:, part] = jnp.dot(perm[...], queries[:, part], preferred_element_type=jnp.float32).astype(jnp.bfloat16)
 
-    def attend(h, i):
+    def block_of(i, j):
+        return i * (i + 1) // 2 + j
+
+    def tiles(n, i, lanes):
+        parts = [kv[n][:, j * slots:(j + 1) * slots, lanes].reshape(keys_in, HD) for j in range(i + 1)]
+        return jnp.concatenate(parts, axis=0)
+
+    def scores(h, i):
         blk = queries[i * slots:(i + 1) * slots, h * G * HD:(h + 1) * G * HD]
         q = jnp.concatenate([blk[:, g * HD:(g + 1) * HD] for g in range(G)], axis=0)
-
-        def tiles(lanes):
-            parts = [kv[h, :, j * slots:(j + 1) * slots, lanes].reshape(keys_in, HD) for j in range(i + 1)]
-            return jnp.concatenate(parts, axis=0)
-
-        s = lax.dot_general(q, tiles(slice(0, HD)), (((1,), (1,)), ((), ())), preferred_element_type=jnp.float32)
+        keys = tiles(h, i, slice(0, HD) if h == 0 else slice(HD, 2 * HD))
+        s = lax.dot_general(q, keys, (((1,), (1,)), ((), ())), preferred_element_type=jnp.float32)
         top = None
         for j in range(i + 1):
             t = s[:, j * keys_in:(j + 1) * keys_in].reshape(G, slots, keys_in)
             t = jnp.minimum(t, bias[j, i * slots:(i + 1) * slots, :][None]).reshape(m, keys_in)
-            held[j] = t
+            held[block_of(i, j)] = t
             most = jnp.maximum(jnp.maximum(t[:, :HD], t[:, HD:2 * HD]), jnp.maximum(t[:, 2 * HD:3 * HD], t[:, 3 * HD:]))
             top = most if top is None else jnp.maximum(top, most)
-        low = jnp.max(top, axis=1, keepdims=True) * shift
-        w = jnp.concatenate([jnp.exp2(held[j] * shift - low).astype(jnp.bfloat16) for j in range(i + 1)], axis=1)
-        value = tiles(slice(HD, 2 * HD))
-        acc = jnp.dot(w, jnp.concatenate([value, jnp.ones_like(value)], axis=1), preferred_element_type=jnp.float32)
+        tops[i] = top
+
+    def weigh(h, i):
+        low = jnp.max(tops[i], axis=1, keepdims=True) * shift
+        w = [jnp.exp2(held[block_of(i, j)] * shift - low).astype(jnp.bfloat16) for j in range(i + 1)]
+        value = tiles(h + 1, i, slice(0, HD))
+        value = jnp.concatenate([value, jnp.ones_like(value)], axis=1)
+        acc = jnp.dot(jnp.concatenate(w, axis=1), value, preferred_element_type=jnp.float32)
         res = (acc[:, :HD] / acc[:, HD:]).astype(jnp.bfloat16)
         part = pl.ds(i * slots, slots)
         rows_out[part, :] = jnp.concatenate([res[g * slots:(g + 1) * slots] for g in range(G)], axis=1)
@@ -282,7 +300,7 @@
     steps = {
         "z": ring, "h": cross, "o": crossed, "E": share_own, "f": share_other, "p": project,
         "K": lambda h, side: spread(h, yhi, 1, side), "L": kv_partner,
-        "M": lambda h, side: spread(h, 1 - yhi, 5, side), "Q": kv_far, "N": kv_last, "A": attend,
+        "M": lambda h, side: spread(h, 1 - yhi, 5, side), "Q": kv_far, "N": kv_last, "S": scores, "V": weigh,
     }
     plain = {"n": norm, "r": order, "m": masks, "q": sort_queries}
     for item in ORDER:
@@ -318,9 +336,11 @@
             pltpu.VMEM(position.shape, jnp.int32),
             pltpu.VMEM(k_weight.shape, half),
             pltpu.VMEM(v_weight.shape, half),
-            pltpu.VMEM((KVH, Z, 2, 2, rows, 2 * HD), half),
+            pltpu.VMEM((2, Z, 2, 2, rows, HD), half),
+            pltpu.VMEM((KVH - 1, Z, 2, 2, rows, 2 * HD), half),
             pltpu.VMEM((tokens, features), half),
-            pltpu.VMEM((KVH, GROUPS, tokens, 2 * HD), half),
+            pltpu.VMEM((2, GROUPS, tokens, HD), half),
+            pltpu.VMEM((KVH - 1, GROUPS, tokens, 2 * HD), half),
             pltpu.VMEM((GROUPS, 1, tokens), jnp.int32),
             pltpu.VMEM((tokens, tokens), half),
             pltpu.VMEM((tokens, tokens), half),
@@ -328,13 +348,14 @@
             pltpu.VMEM((tokens, HD), full),
             pltpu.VMEM((tokens, HD), jnp.int32),
             pltpu.VMEM((TILES, tokens, keys_in), full),
-            pltpu.VMEM((TILES, m, keys_in), full),
+            pltpu.VMEM((TILES * (TILES + 1) // 2, m, keys_in), full),
+            pltpu.VMEM((TILES, m, HD), full),
             pltpu.VMEM((tokens, G * HD), half),
             pltpu.VMEM((KVH, tokens, G * HD), half),
             dma((8,)),
-            dma((KVH, 2, 4)), dma((KVH, 2, 4)), dma((KVH, 2)), dma((KVH, 2)), dma((KVH, 2)), dma((KVH, 2)),
-            dma((KVH, 2, 4)), dma((KVH, 2, 4)), dma((KVH, 2)), dma((KVH, 2)),
-            dma((KVH, 10)), dma((KVH, 10)), dma((7,)), dma((7,)), dma((KVH,)),
+            dma((PARTS, 2, 4)), dma((PARTS, 2, 4)), dma((PARTS, 2)), dma((PARTS, 2)), dma((PARTS, 2)), dma((PARTS, 2)),
+            dma((PARTS, 2, 4)), dma((PARTS, 2, 4)), dma((PARTS, 2)), dma((PARTS, 2)),
+            dma((PARTS, 10)), dma((PARTS, 10)), dma((7,)), dma((7,)), dma((KVH,)),
         ],
         compiler_params=pltpu.CompilerParams(collective_id=0, has_side_effects=True, vmem_limit_bytes=60 * 2**20),
         cost_estimate=pl.CostEstimate(flops=12 * 10**9, bytes_accessed=10**8, transcendentals=2 * 10**7),

time: 86.3 us -> 82.3 us (0.954)
  Pallas kernels: 83.1 us -> 79.1 us
    pallas_call x1, Pallas kernels: 83.1 us -> 79.1 us  [fused(): pl.pallas_call(fused_kernel, out_shape=jax.ShapeDtypeStruct(queries.shape...]
where the time goes in v3:
time: 82.3 us; the launch traced here: 82.2 us
  Pallas kernels  79.1 us (96%)
  local copies, waits for them, and re-layouts  3.13 us (4%)
    pallas_call x1, Pallas kernels, fused(): pl.pallas_call(fused_kernel, out_shape=jax.ShapeDtypeStruct(queries.shape...  79.1 us
    unnamed x1, local copies, waits for them, and re-layouts  3.13 us

profile of v3, /device:TPU:1, one launch (start us, length us, event | category | flops | bytes accessed | tf_op | source)
XLA Modules:
  0.0 82.2 jit_solution(1066316564786153428)
XLA Ops:
  0.0 79.1 %project_gather_attend.1 = bf16[256,4096]{1,0:T(8,128)(2,1)} custom-call(bf16[256,5120]{1,0:T(8,128)(2,1)} %bitcast.6, bf16[256,4096]{1,0:T(8,128)(2,1)} %bitcast.7, f32[1,5120]{1,0:T(1,128)} %bitcast.8, f32[1,128]{1,0:T(1,128)} %bitcast.9, s32[1,256]{1,0:T(1,128)} %segment_hbm.1, s32[1,256]{1,0:T(1,128)} %position_hbm.1, bf16[160,512]{1,0:T(8,128)(2,1)} %kw_hbm.1, ...), custom_call_target="tpu_custom_call" | custom-call | flops 12000000000 | bytes 100000000 | tf_op jit(solution)/shard_map/project_gather_attend/pallas_call | solution.py:325
  79.1 3.1 %copy.10 = bf16[1,256,4096]{2,1,0:T(8,128)(2,1)} copy(bf16[1,256,4096]{2,1,0:T(8,128)(2,1)} %bitcast.5) | data formatting | bytes 4194304

commit v4 on v3

--- a/solution.py
+++ b/solution.py
@@ -33,19 +33,20 @@
 
 
 ORDER = (
-    "z100", "z110", "z200", "z210", "h2", "z000", "h1", "h4", "z010", "h0", "z310", "z101", "o1", "z201", "h3",
-    "z111", "z001", "r", "z102", "z211", "q", "z410", "z011", "o0", "z300", "z002", "z112", "z103", "z202", "z212",
-    "m", "n", "z012", "z104", "z113", "z003", "z301", "z203", "z013", "z400", "E1", "z411", "z311", "f1", "z004",
-    "z213", "z302", "E0", "z412", "p1", "z312", "f0", "z401", "z204", "o2", "p0", "z303", "o4", "z313", "E2", "o3",
-    "L1", "f2", "z413", "K11", "K00", "z304", "K10", "K01", "z402", "E3", "p2", "M10", "M11", "z403", "f3", "Q0",
-    "Q1", "L0", "K21", "z404", "K20", "p3", "M00", "L2", "M01", "Q2", "E4", "N0", "S00", "S01", "S02", "S03", "N1",
-    "V00", "f4", "V01", "K31", "K30", "S11", "S10", "p4", "V02", "V03", "M20", "M21", "L3", "Q3", "S13", "N2",
-    "V10", "K40", "K41", "V11", "S12", "S20", "V12", "V13", "S21", "L4", "M31", "S23", "M30", "Q4", "N3", "V20",
-    "V21", "S22", "V22", "S31", "V23", "M40", "S32", "M41", "S30", "N4", "S33", "V30", "V31", "V32", "V33",
+    "z000", "z210", "z010", "h4", "h0", "z100", "h1", "z310", "z300", "h3", "z001", "z110", "z200", "r", "h2",
+    "z011", "z211", "z101", "z002", "n", "o1", "z111", "z410", "z201", "z102", "z003", "z112", "z012", "z202",
+    "z103", "z301", "m", "z212", "z400", "q", "z311", "z004", "z411", "o0", "z113", "z013", "z203", "z104", "z312",
+    "z302", "z401", "f0", "E0", "o2", "o3", "z412", "z213", "E1", "z204", "f1", "p0", "z303", "p1", "K00", "E2",
+    "z402", "K01", "o4", "f2", "L0", "z304", "z403", "z313", "E3", "K11", "K10", "z413", "Q0", "L1", "p2", "f3",
+    "z404", "Q1", "M00", "p3", "M01", "M10", "f4", "E4", "M11", "K20", "N0", "S01", "S02", "K21", "L2", "S00", "p4",
+    "N1", "K31", "V00", "K30", "V01", "Q2", "S03", "L3", "V02", "V03", "S11", "S10", "M20", "S13", "S12", "L4",
+    "K41", "M21", "Q3", "N2", "V10", "K40", "V11", "S21", "V12", "S22", "V13", "S23", "S20", "M31", "M41", "M30",
+    "M40", "Q4", "N3", "V20", "V21", "S31", "V22", "S30", "V23", "S33", "S32", "N4", "V30", "V31", "V32", "V33",
 )
 PARTS = KVH + 1
 BY_Y = (0, 1, 2, 3, 4)
-ALL_Y = (0, 1, 2)
+ALL_Y = (0, 1)
+DIRECT = ()
 
 
 def fused_kernel(
@@ -72,7 +73,9 @@
     loads = [pltpu.make_async_copy(a, b, in_sem.at[n]) for n, (a, b) in enumerate(((kw_hbm, kw), (vw_hbm, vw), (segment_hbm, segment_ref), (position_hbm, position_ref), (key_gain_hbm, key_gain_ref), (gain_hbm, gain_ref), (hidden_hbm, hidden), (queries_hbm, queries)))]
     for load in loads:
         load.start()
-    peers = [(x + dx, y + dy, z, core) for dx in range(X) for dy in (0, 2) if (dx, dy) != (0, 0)]
+    ways = [(dx, 0) for dx in (1, -1, 2)] + [(dx, 2) for dx in (0, 1, -1, 2)]
+    peers = [(x + dx, y + dy, z, core) for dx, dy in ways]
+    origins = [((x - dx + X) % X) * 2 + (yhi + dy // 2) % 2 for dx, dy in ways]
     near = [(x, y, z + 1, core), (x, y, z - 1, core), (x, y + 1, z, core), (x, y - 1, z, core), (x, y, z, 1 - core)]
     barrier = pltpu.get_barrier_semaphore()
     for at in near + peers:
@@ -170,6 +173,10 @@
         both = jnp.concatenate(made, axis=1)
         kv[h][ctx] = jnp.dot(perm[...], both, preferred_element_type=jnp.float32).astype(jnp.bfloat16)
         block = kv[h].at[ctx]
+        if h in DIRECT:
+            for n in reversed(range(len(peers))):
+                kv_send_to(h, n, block, peers[n])
+            return
         kv_send_to(h, 0, block, (x, y + 2, z, core))
         kv_send_to(h, 1, block, (x + 1, y, z, core))
         kv_send_to(h, 2, block, (x - 1, y, z, core))
@@ -198,6 +205,10 @@
             kv_send_to(h, 9, far(h, yhi), (x, y + 2, z, core))
 
     def kv_last(h):
+        if h in DIRECT:
+            for n, origin in enumerate(origins):
+                kv_arrived(h, n, kv[h].at[origin])
+            return
         if h in BY_Y:
             kv_arrived(h, 9, far(h, 1 - yhi))
         else:
@@ -234,10 +245,8 @@
         sin[...] = jnp.where(lane < HD // 2, -1.0, 1.0) * jnp.sin(angle)
 
     def masks():
-        for n in range(len(peers)):
-            dx, dy = [(dx, dy) for dx in range(X) for dy in (0, 2) if (dx, dy) != (0, 0)][n]
-            src = ((x + X - dx) % X) * 2 + (yhi + dy // 2) % 2
-            arrived(codes.at[src], c_send.at[n], c_recv.at[n])
+        for n, origin in enumerate(origins):
+            arrived(codes.at[origin], c_send.at[n], c_recv.at[n])
         own = own_code[:, :1]
         start = own // BIG * BIG
         for j in range(TILES):
@@ -306,7 +315,7 @@
     for item in ORDER:
         if item in plain:
             plain[item]()
-        else:
+        elif item[0] not in "KLMQ" or int(item[1]) not in DIRECT:
             steps[item[0]](*[int(digit) for digit in item[1:]])
     for copy in sent:
         copy.wait_send()

time: 82.3 us -> 83.9 us (1.019)
  the two profiles are of different devices: /device:TPU:1 before, /device:TPU:8 now
where the time goes in v4:
time: 83.9 us; the launch traced here: 83.8 us
  Pallas kernels  80.6 us (96%)
  local copies, waits for them, and re-layouts  3.13 us (4%)
    pallas_call x1, Pallas kernels, fused(): pl.pallas_call(fused_kernel, out_shape=jax.ShapeDtypeStruct(queries.shape...  80.6 us
    unnamed x1, local copies, waits for them, and re-layouts  3.13 us

profile of v4, /device:TPU:8, one launch (start us, length us, event | category | flops | bytes accessed | tf_op | source)
XLA Modules:
  0.0 83.8 jit_solution(11286352640998286272)
XLA Ops:
  0.0 80.6 %project_gather_attend.1 = bf16[256,4096]{1,0:T(8,128)(2,1)} custom-call(bf16[256,5120]{1,0:T(8,128)(2,1)} %bitcast.6, bf16[256,4096]{1,0:T(8,128)(2,1)} %bitcast.7, f32[1,5120]{1,0:T(1,128)} %bitcast.8, f32[1,128]{1,0:T(1,128)} %bitcast.9, s32[1,256]{1,0:T(1,128)} %segment_hbm.1, s32[1,256]{1,0:T(1,128)} %position_hbm.1, bf16[160,512]{1,0:T(8,128)(2,1)} %kw_hbm.1, ...), custom_call_target="tpu_custom_call" | custom-call | flops 12000000000 | bytes 100000000 | tf_op jit(solution)/shard_map/project_gather_attend/pallas_call | solution.py:334
  80.6 3.1 %copy.10 = bf16[1,256,4096]{2,1,0:T(8,128)(2,1)} copy(bf16[1,256,4096]{2,1,0:T(8,128)(2,1)} %bitcast.5) | data formatting | bytes 4194304
